TPU v7x, 256 devices: a whole 4x4x8 slice. The times are simulated.
256 devices in a mesh: wide: 64 (over y, z, x_hi), narrow: 4 (over x_lo, core).
Axes of the slice: x: 4 (x_hi: 2, x_lo: 2; x = x_hi * 2 + x_lo), y: 4, z: 8, core: 2. Of those that a mesh axis runs over, the one named last changes fastest.
Arguments:
- phase: float32 [512, 256, 512], P('wide', 'narrow'), may hold values from -6 to 6
- velocity: float32 [512, 256, 512], P('wide', 'narrow'), may hold values from -6 to 6
- basis: float32 [512, 512], replicated, may hold values from -0.25 to 0.25
- dual_basis: float32 [512, 512], replicated, may hold values from -0.25 to 0.25
- wall_slope: float32 [512, 512], replicated, may hold values from -0.25 to 0.25
- decay_rates: float32 [512], replicated, may hold values from 0.25 to 4
Outputs:
- new_phase: float32 [512, 256, 512], P('wide', 'narrow')
- new_velocity: float32 [512, 256, 512], P('wide', 'narrow')
All inputs are finite; a program needn't handle non-finite values.
Results may differ from a plain program's by a relative error of at most 0.00005.
Values sent between devices are 32-bit elements; how exact they have to be, the bound alone decides.
No kernel may reach another device: no remote copies, remote signals or barrier semaphores. Data moves between devices by JAX's collectives and lax.ppermute only.
A program may use at most 128 MiB of HBM per device.

v0:
```python
import functools
import math

import jax
import jax.numpy as jnp
import ml_dtypes
import numpy as np
from jax import lax
from jax.experimental import pallas as pl
from jax.experimental.pallas import tpu as pltpu
from jax.sharding import PartitionSpec as P

time_step = 0.1
mobility = 0.5
stabilize = 1.0
interface_sq = 0.25
capillary = 0.5
viscosity = 0.3

f32 = jnp.float32
bf16 = jnp.bfloat16


def wavenumber(length):
    indices = np.arange(length)
    return np.where(indices < length // 2, indices, indices - length) * (2.0 / length)


def tables(length):
    indices = np.arange(length)
    angles = (indices[:, None] * indices[None, :] % length) * (2.0 * math.pi / length)
    scaling = 1.0 / math.sqrt(length)
    cas_table = (np.cos(angles) + np.sin(angles)) * scaling
    slope_table = wavenumber(length)[None, :] * (np.cos(angles) - np.sin(angles)) * scaling
    return cas_table, slope_table


def halves(table):
    high = table.astype(np.float32).astype(ml_dtypes.bfloat16)
    low = (table - high.astype(np.float64)).astype(np.float32).astype(ml_dtypes.bfloat16)
    return np.stack([high, low])


def span_tables(length):
    cas, slope = tables(length)
    return np.stack([halves(cas.T), halves(slope.T), halves(-slope)])


def stream_tables(length, wide):
    cas, slope = tables(length)
    half = length // 2
    order = np.arange(half).reshape(wide, half // wide).T.reshape(half)
    ahead = [table[:half, parity::2][:, order] for table in (cas, slope) for parity in range(2)]
    back = [table[parity::2, :half][order] for table in (cas, -slope.T) for parity in range(2)]
    return np.stack([halves(t) for t in ahead + back])


def split(value):
    high = value.astype(bf16)
    return high, (value - high.astype(f32)).astype(bf16)


def dot3(left, right):
    def dot(a, b):
        return jnp.dot(a, b, preferred_element_type=f32)

    return dot(left[0], right[0]) + (dot(left[0], right[1]) + dot(left[1], right[0]))


def wave_squared(column, width, rows_x, rows_z, full_x, full_z):
    at = lax.broadcasted_iota(jnp.int32, (1, width), 1) + column

    def squared(first, own, length):
        index = first + own
        signed = jnp.where(index < length // 2, index, index - length)
        return (signed.astype(f32) * (2.0 / length)) ** 2

    return squared(lax.axis_index("wide") * rows_x, at // rows_z, full_x) + squared(
        lax.axis_index("narrow") * rows_z, at % rows_z, full_z
    )


def upright(decay_ref, width):
    turned = jnp.broadcast_to(decay_ref[...], (128, decay_ref.shape[1])).T
    return jnp.concatenate([turned] * (width // 128), axis=1)


def fetch(sources, targets, sems):
    copies = [pltpu.make_async_copy(s, t, sems.at[at]) for at, (s, t) in enumerate(zip(sources, targets))]
    for copy in copies:
        copy.start()
    return copies


def field_rows(ref, field):
    held = ref.at[field]
    return held.reshape(held.shape[0] * held.shape[1], held.shape[2])


def of_field(ref, field):
    return ref.at[:, field * 8 : field * 8 + 8]


def eigen_kernel(sizes, phase_in, dual_in, slope_in, basis_in, decay_in, send_out, eig_out, *scratch):
    send_ref, phase_ref, dual_ref, slope_ref, basis_ref, decay_ref, eig_ref, sems = scratch
    levels = phase_ref.shape[1]
    half = levels // 2
    width = 256
    columns = range(0, phase_ref.shape[0], width)
    first, second = (pl.ds(column, width) for column in columns)
    copies = fetch(
        [phase_in.at[first], phase_in.at[second], dual_in, slope_in, basis_in, decay_in],
        [phase_ref.at[first], phase_ref.at[second], dual_ref, slope_ref, basis_ref, decay_ref],
        sems,
    )
    done = []

    def leave(source, target):
        done.append(pltpu.make_async_copy(source, target, sems.at[6 + len(done)]))
        done[-1].start()

    def put(field, values):
        rows = field_rows(send_ref, field)
        for column, value in zip(columns, values):
            for block in range(width // 128):
                for level in range(2):
                    row = (column // 128 + block) * 2 + level
                    rows[pl.ds(row, half, stride=8), :] = value[
                        level * half : (level + 1) * half, block * 128 : (block + 1) * 128
                    ]
        leave(send_ref.at[field], of_field(send_out, field))

    turned = []
    for at, column in enumerate(columns):
        copies[at].wait()
        turned.append(phase_ref[column : column + width, :].T)
    put(0, turned)
    pairs = [split(value) for value in turned]
    copies[2].wait()
    dual = split(dual_ref[...])
    eig = [dot3(dual, pair) for pair in pairs]
    for column, value in zip(columns, eig):
        eig_ref[:, column : column + width] = value
    leave(eig_ref, eig_out)
    copies[3].wait()
    slope = split(slope_ref[...])
    put(1, [dot3(slope, pair) for pair in pairs])
    copies[4].wait()
    copies[5].wait()
    basis = split(basis_ref[...])
    decay = upright(decay_ref, width)
    put(
        2,
        [
            dot3(basis, split(-(decay + wave_squared(column, width, *sizes)) * value))
            for column, value in zip(columns, eig)
        ],
    )
    for copy in done:
        copy.wait()


def velocity_kernel(velocity_ref, dual_ref, slope_ref, basis_ref, eig_ref, pairs_ref):
    dual = split(dual_ref[...])
    width = 256
    for column in range(0, velocity_ref.shape[0], width):
        eig_ref[:, column : column + width] = dot3(dual, split(velocity_ref[column : column + width, :].T))
        slope = dot3(dual, split(slope_ref[:, column : column + width]))
        pairs_ref[1, 0, :, column : column + width], pairs_ref[1, 1, :, column : column + width] = split(-slope)
    pairs_ref[0, 0], pairs_ref[0, 1] = dual
    pairs_ref[2, 0], pairs_ref[2, 1] = split(basis_ref[...])


def plane_kernel(wide, narrow, recv_in, span_in, stream_in, send_out, recv_ref, send_ref, span_ref, stream_ref, sems):
    copies = fetch(
        [of_field(recv_in, 0), span_in, stream_in, of_field(recv_in, 1), of_field(recv_in, 2)],
        [recv_ref.at[0], span_ref, stream_ref, recv_ref.at[1], recv_ref.at[2]],
        sems,
    )
    done = []

    def arrive(level, *which):
        if level == 0:
            for at in which:
                copies[at].wait()

    def pair(ref):
        return ref[0], ref[1]

    lower = lax.broadcasted_iota(jnp.int32, (4 * wide, 128), 1) < 64

    def rows(n, block, level):
        return pl.ds(n * wide * 8 + block * 2 + level, wide, stride=8)

    def load(field, level):
        held = field_rows(recv_ref, field)
        parts = [
            jnp.concatenate([held[rows(n, block, level), :] for block in range(4)], axis=0)
            for n in range(narrow)
        ]
        turned = [pltpu.roll(part, 64, 1) for part in parts]
        even = [jnp.where(lower, parts[n], turned[n + 1]) for n in range(0, narrow, 2)]
        odd = [jnp.where(lower, turned[n], parts[n + 1]) for n in range(0, narrow, 2)]
        return split(jnp.concatenate(even, axis=1)), split(jnp.concatenate(odd, axis=1))

    def one_level(level):
        def across(field, at):
            return tuple(split(dot3(part, pair(span_ref.at[at]))) for part in field)

        def ahead(field, at):
            first = dot3(pair(stream_ref.at[2 * at]), field[0])
            second = dot3(pair(stream_ref.at[2 * at + 1]), field[1])
            return first + second, first - second

        arrive(level, 0)
        phase = load(0, level)
        arrive(level, 1, 2)
        spread = across(phase, 0)
        value, grad_x = ahead(spread, 0), ahead(spread, 1)
        grad_z = ahead(across(phase, 1), 0)
        arrive(level, 3, 4)
        grad_y = ahead(across(load(1, level), 0), 0)
        lap = ahead(across(load(2, level), 0), 0)
        explicit, force_x, force_y, force_z = [], [], [], []
        for part in range(2):
            v = value[part]
            cubed = v * v * v
            push = capillary * (cubed - v - interface_sq * lap[part])
            explicit.append(cubed - (1.0 + stabilize) * v)
            force_x.append(push * grad_x[part])
            force_y.append(push * grad_y[part])
            force_z.append(push * grad_z[part])

        def back(value, at):
            folded = value[0] + value[1], value[0] - value[1]
            return tuple(
                split(dot3(pair(stream_ref.at[4 + 2 * at + parity]), split(folded[parity]))) for parity in range(2)
            )

        def put(field, even, odd):
            held = field_rows(send_ref, field)
            for n in range(0, narrow, 2):
                here = slice(n * 64, n * 64 + 128)
                first, second = even[:, here], odd[:, here]
                for own, value in (
                    (n, jnp.where(lower, first, pltpu.roll(second, 64, 1))),
                    (n + 1, jnp.where(lower, pltpu.roll(first, 64, 1), second)),
                ):
                    for block in range(4):
                        held[rows(own, block, level), :] = value[block * wide : (block + 1) * wide]
            if level == 1:
                done.append(pltpu.make_async_copy(send_ref.at[field], of_field(send_out, field), sems.at[5 + field]))
                done[-1].start()

        put(0, *[dot3(part, pair(span_ref.at[0])) for part in back(explicit, 0)])
        put(1, *[dot3(part, pair(span_ref.at[0])) for part in back(force_y, 0)])
        put(
            2,
            *[
                dot3(a, pair(span_ref.at[0])) + dot3(b, pair(span_ref.at[2]))
                for a, b in zip(back(force_x, 1), back(force_z, 0))
            ],
        )

    for level in range(2):
        one_level(level)
    for copy in done:
        copy.wait()


def update_kernel(sizes, recv_in, eig_in, velocity_in, pairs_in, decay_in, phase_out, velocity_out, *scratch):
    recv_ref, eig_ref, velocity_ref, pairs_ref, decay_ref, phase_ref, result_ref, sems = scratch
    copies = fetch(
        [of_field(recv_in, 0), pairs_in.at[0], of_field(recv_in, 1), of_field(recv_in, 2)]
        + [pairs_in.at[1], decay_in, eig_in, velocity_in, pairs_in.at[2]],
        [recv_ref.at[0], pairs_ref.at[0], recv_ref.at[1], recv_ref.at[2]]
        + [pairs_ref.at[1], decay_ref, eig_ref, velocity_ref, pairs_ref.at[2]],
        sems,
    )
    half = eig_ref.shape[0] // 2
    width = 256
    columns = range(0, eig_ref.shape[1], width)

    def get(field, column):
        rows = field_rows(recv_ref, field)
        return jnp.concatenate(
            [
                jnp.concatenate(
                    [
                        rows[pl.ds((column // 128 + block) * 2 + level, half, stride=8), :]
                        for block in range(width // 128)
                    ],
                    axis=1,
                )
                for level in range(2)
            ],
            axis=0,
        )

    def pair(at):
        return pairs_ref[at, 0], pairs_ref[at, 1]

    explicit, forcing = [], []
    for column in columns:
        if column == 0:
            copies[0].wait()
        value = split(get(0, column))
        if column == 0:
            copies[1].wait()
        explicit.append(dot3(pair(0), value))
        wave = wave_squared(column, width, *sizes)
        if column == 0:
            for copy in copies[2:5]:
                copy.wait()
        value = split(-wave * get(1, column))
        other = split(get(2, column))
        forcing.append(dot3(pair(0), value) + dot3(pair(1), other))
    for copy in copies[5:]:
        copy.wait()
    decay = upright(decay_ref, width)
    done = []
    for at, column in enumerate(columns):
        here = slice(column, column + width)
        operator = -(decay + wave_squared(column, width, *sizes))
        damping = 1.0 + time_step * mobility * -operator * (stabilize + interface_sq * -operator)
        phase = (eig_ref[:, here] + time_step * mobility * operator * explicit[at]) / damping
        velocity = (operator * velocity_ref[:, here] + time_step * forcing[at]) / (
            operator * (1.0 - time_step * viscosity * operator)
        )
        for which, (value, ref, out) in enumerate(
            ((phase, phase_ref, phase_out), (velocity, result_ref, velocity_out))
        ):
            ref[here, :] = dot3(pair(2), split(value)).T
            done.append(pltpu.make_async_copy(ref.at[here], out.at[here], sems.at[9 + 2 * at + which]))
            done[-1].start()
    for copy in done:
        copy.wait()


hbm = pl.BlockSpec(memory_space=pltpu.HBM)
vmem = pl.BlockSpec(memory_space=pltpu.VMEM)


def call(kernel, ins, outs, shapes, scratch, flops, limit):
    return pl.pallas_call(
        kernel,
        out_shape=shapes,
        in_specs=ins,
        out_specs=outs,
        scratch_shapes=scratch,
        compiler_params=pltpu.CompilerParams(vmem_limit_bytes=limit << 20),
        cost_estimate=pl.CostEstimate(flops=flops, bytes_accessed=4 << 20, transcendentals=0),
    )


def stages(rows_x, rows_z, levels, wide, narrow):
    full_x, full_z = rows_x * wide, rows_z * narrow
    count = rows_x * rows_z
    sizes = rows_x, rows_z, full_x, full_z
    square = jax.ShapeDtypeStruct((levels, count), f32)
    flat = jax.ShapeDtypeStruct((wide * narrow, 24, 128), f32)
    buffer = pltpu.VMEM((3, wide * narrow, 8, 128), f32)
    pairs = jax.ShapeDtypeStruct((3, 2, levels, levels), bf16)
    held, line = pltpu.VMEM((levels, count), f32), pltpu.VMEM((1, levels), f32)
    sems = pltpu.SemaphoreType.DMA
    first = call(
        functools.partial(eigen_kernel, sizes),
        [hbm] * 5,
        [hbm, hbm],
        [flat, square],
        [buffer] + [held] * 4 + [line, held, sems((10,))],
        3 * 6 * 512**3,
        60,
    )
    beside = call(velocity_kernel, [vmem] * 4, [vmem] * 2, [square, pairs], [], 2 * 6 * 512**3, 24)
    span, stream = (jnp.asarray(t) for t in (span_tables(full_z), stream_tables(full_x, wide)))
    planes = call(
        functools.partial(plane_kernel, wide, narrow),
        [hbm] * 3,
        hbm,
        flat,
        [buffer, buffer, pltpu.VMEM(span.shape, bf16), pltpu.VMEM(stream.shape, bf16), sems((8,))],
        204 * 2 * 256**3,
        60,
    )
    last = call(
        functools.partial(update_kernel, sizes),
        [hbm] * 5,
        [hbm] * 2,
        [square] * 2,
        [buffer] + [held] * 2
        + [pltpu.VMEM(pairs.shape, bf16), line, held, held, sems((13,))],
        5 * 6 * 512**3,
        60,
    )
    return first, beside, lambda recv: planes(recv, span, stream), last


def body(phase, velocity, basis, dual_basis, wall_slope, decay_rates):
    rows_x, rows_z, levels = phase.shape
    wide, narrow = lax.axis_size("wide"), lax.axis_size("narrow")
    first, beside, planes, last = stages(rows_x, rows_z, levels, wide, narrow)
    decay = decay_rates.reshape(1, levels)

    def exchange(parts):
        return lax.all_to_all(parts, ("narrow", "wide"), split_axis=0, concat_axis=0, tiled=True)

    send, phase_eig = first(phase.reshape(-1, levels), dual_basis, wall_slope, basis, decay)
    velocity_eig, pairs = beside(velocity.reshape(-1, levels), dual_basis, wall_slope, basis)
    recv = exchange(send)
    recv, velocity_eig, pairs = lax.optimization_barrier((recv, velocity_eig, pairs))
    recv = exchange(planes(recv))
    outs = last(recv, phase_eig, velocity_eig, pairs, decay)
    return tuple(out.reshape(phase.shape) for out in outs)


def solution(mesh):
    return jax.shard_map(
        body,
        mesh=mesh,
        in_specs=(P("wide", "narrow", None), P("wide", "narrow", None), P(), P(), P(), P()),
        out_specs=(P("wide", "narrow", None), P("wide", "narrow", None)),
        check_vma=False,
    )
```

profile of v0, /device:TPU:32, one launch (start us, length us, event | category | flops | bytes accessed | tf_op | source)
XLA Modules:
  0.0 201.3 jit_solution(13429374433789655189)
XLA Ops:
  0.6 6.1 %shard_map.95 = (f32[256,24,128]{2,1,0:T(8,128)}, f32[512,512]{1,0:T(8,128)}) custom-call(f32[512,512]{1,0:T(8,128)} %bitcast.6, f32[512,512]{1,0:T(8,128)} %dual_ref.1, f32[512,512]{1,0:T(8,128)} %slope_ref.1, f32[512,512]{1,0:T(8,128)} %basis_ref.1, f32[1,512]{1,0:T(1,128)} %bitcast.7), custom_call_target="tpu_custom_call" | custom-call | flops 2415919104 | bytes 4194304 | tf_op jit(solution)/shard_map/pallas_call | solution.py:408
  6.7 0.0 copy-start
  6.7 0.0 copy-start.1
  6.8 0.0 copy-start.2
  6.8 15.3 %all-to-all-start = ((f32[256,24,128]{2,1,0:T(8,128)}), f32[256,24,128]{2,1,0:T(8,128)}, u32[]{:S(2)}, u32[]{:S(2)}) async-start(f32[256,24,128]{2,1,0:T(8,128)} %get-tuple-element.11), calls=%async_computation | async-start | bytes 6291456 | tf_op jit(solution)/shard_map/all_to_all | solution.py:406
  22.1 0.0 copy-done
  22.1 0.0 copy-done.1
  22.1 0.0 copy-done.2
  22.1 0.0 copy-start.3
  22.1 1.2 copy-done.3
  23.3 2.1 %shard_map.96 = (f32[512,512]{1,0:T(8,128)S(1)}, bf16[3,2,512,512]{3,2,1,0:T(8,128)(2,1)S(1)}) custom-call(f32[512,512]{1,0:T(8,128)S(1)} %bitcast.5, f32[512,512]{1,0:T(8,128)S(1)} %copy-done, f32[512,512]{1,0:T(8,128)S(1)} %copy-done.1, f32[512,512]{1,0:T(8,128)S(1)} %copy-done.2), custom_call_target="tpu_custom_call" | custom-call | flops 1610612736 | bytes 4194304 | tf_op jit(solution)/shard_map/pallas_call | solution.py:409
  25.5 0.0 copy-start.4
  25.5 1.6 copy-done.4
  27.1 0.0 copy-start.5
  27.1 1.0 copy-done.5
  28.1 68.6 %all-to-all-done.recv_in = f32[256,24,128]{2,1,0:T(8,128)} async-done(((f32[256,24,128]{2,1,0:T(8,128)}), f32[256,24,128]{2,1,0:T(8,128)}, u32[]{:S(2)}, u32[]{:S(2)}) %all-to-all-start) | async-done | bytes 3145760 | tf_op jit(solution)/shard_map/all_to_all | solution.py:406
  96.7 12.9 %shard_map.97 = f32[256,24,128]{2,1,0:T(8,128)} custom-call(f32[256,24,128]{2,1,0:T(8,128)} %all-to-all-done.recv_in, bf16[3,2,256,256]{3,2,1,0:T(8,128)(2,1)} %constant.4.clone.span_in, bf16[8,2,256,256]{3,2,1,0:T(8,128)(2,1)} %constant.5.clone.stream_in), custom_call_target="tpu_custom_call" | custom-call | flops 6845104128 | bytes 4194304 | tf_op jit(solution)/shard_map/pallas_call | solution.py:396
  109.6 82.1 %all_to_all.10.recv_in = f32[256,24,128]{2,1,0:T(8,128)} all-to-all(f32[256,24,128]{2,1,0:T(8,128)} %shard_map.97), channel_id=1, replica_groups=mesh['wide'=64,'narrow'=4] {'narrow','wide'}, dimensions={0} | all-to-all | bytes 6291456 | tf_op jit(solution)/shard_map/all_to_all | solution.py:406
  191.7 9.5 %shard_map.98 = (f32[512,512]{1,0:T(8,128)}, f32[512,512]{1,0:T(8,128)}) custom-call(f32[256,24,128]{2,1,0:T(8,128)} %all_to_all.10.recv_in, f32[512,512]{1,0:T(8,128)} %get-tuple-element.15.eig_in, f32[512,512]{1,0:T(8,128)} %copy-done.5, bf16[3,2,512,512]{3,2,1,0:T(8,128)(2,1)} %copy-done.4, f32[1,512]{1,0:T(1,128)} %bitcast.8), custom_call_target="tpu_custom_call" | custom-call | flops 4026531840 | bytes 4194304 | tf_op jit(solution)/shard_map/pallas_call | solution.py:413
Async XLA Ops:
  6.7 15.3 %copy-start = (f32[512,512]{1,0:T(8,128)S(1)}, f32[512,512]{1,0:T(8,128)}, u32[]{:S(2)}) copy-start(f32[512,512]{1,0:T(8,128)} %dual_ref.1) | copy-start | bytes 3145732
  6.7 15.3 %copy-start.1 = (f32[512,512]{1,0:T(8,128)S(1)}, f32[512,512]{1,0:T(8,128)}, u32[]{:S(2)}) copy-start(f32[512,512]{1,0:T(8,128)} %slope_ref.1) | copy-start | bytes 3145732
  6.8 15.3 %copy-start.2 = (f32[512,512]{1,0:T(8,128)S(1)}, f32[512,512]{1,0:T(8,128)}, u32[]{:S(2)}) copy-start(f32[512,512]{1,0:T(8,128)} %basis_ref.1) | copy-start | bytes 3145732
  6.8 89.9 %all-to-all-start = ((f32[256,24,128]{2,1,0:T(8,128)}), f32[256,24,128]{2,1,0:T(8,128)}, u32[]{:S(2)}, u32[]{:S(2)}) async-start(f32[256,24,128]{2,1,0:T(8,128)} %get-tuple-element.11), calls=%async_computation | async-start | bytes 6291456 | tf_op jit(solution)/shard_map/all_to_all | solution.py:406
  22.1 1.2 copy-start.3
  25.5 1.6 copy-start.4
  27.1 1.0 copy-start.5
where the time goes:
time: 202 us; the launch traced here: 201 us
  blocking collectives  82.1 us (41%)
  waiting for transfers between devices  68.6 us (34%)
  Pallas kernels  30.6 us (15%)
  starting transfers between devices  15.3 us (8%)
  local copies, waits for them, and re-layouts  3.85 us (2%)
    all_to_all x1, blocking collectives, exchange(): lax.all_to_all(parts, ('narrow', 'wide'), split_axis=0, concat_axis=0, ti...  82.1 us
    all_to_all x1, waiting for transfers between devices, exchange(): lax.all_to_all(parts, ('narrow', 'wide'), split_axis=0, concat_axis=0, ti...  68.6 us
    all_to_all x1, starting transfers between devices, exchange(): lax.all_to_all(parts, ('narrow', 'wide'), split_axis=0, concat_axis=0, ti...  15.3 us
    pallas_call x1, Pallas kernels, stages(): return (first, beside, lambda recv: planes(recv, span, stream), last)  12.9 us
    pallas_call x1, Pallas kernels, body(): outs = last(recv, phase_eig, velocity_eig, pairs, decay)  9.45 us
    pallas_call x1, Pallas kernels, body(): first(phase.reshape(-1, levels), dual_basis, wall_slope, basis, decay)  6.1 us
  transfers between devices with their start and end apart: 1, of which 1 were waited for; matrix products, arithmetic and copies ran while one was open for 0% of the time, Pallas kernels for 1%

commit v1 on v0

--- a/solution.py
+++ b/solution.py
@@ -97,26 +97,32 @@
     return held.reshape(held.shape[0] * held.shape[1], held.shape[2])
 
 
+def flat_rows(ref):
+    return ref.reshape(ref.shape[0] * ref.shape[1], ref.shape[2])
+
+
 def of_field(ref, field):
     return ref.at[:, field * 8 : field * 8 + 8]
 
 
-def eigen_kernel(sizes, phase_in, dual_in, slope_in, basis_in, decay_in, send_out, eig_out, *scratch):
-    send_ref, phase_ref, dual_ref, slope_ref, basis_ref, decay_ref, eig_ref, sems = scratch
+def eigen_kernel(
+    sizes, phase_in, velocity_in, dual_in, slope_in, basis_in, decay_in, send_out, eig_out, velocity_out, *scratch
+):
+    send_ref, phase_ref, velocity_ref, dual_ref, slope_ref, basis_ref, decay_ref, eig_ref, other_ref, sems = scratch
     levels = phase_ref.shape[1]
     half = levels // 2
     width = 256
     columns = range(0, phase_ref.shape[0], width)
     first, second = (pl.ds(column, width) for column in columns)
     copies = fetch(
-        [phase_in.at[first], phase_in.at[second], dual_in, slope_in, basis_in, decay_in],
-        [phase_ref.at[first], phase_ref.at[second], dual_ref, slope_ref, basis_ref, decay_ref],
+        [phase_in.at[first], phase_in.at[second], dual_in, slope_in, basis_in, decay_in, velocity_in],
+        [phase_ref.at[first], phase_ref.at[second], dual_ref, slope_ref, basis_ref, decay_ref, velocity_ref],
         sems,
     )
     done = []
 
     def leave(source, target):
-        done.append(pltpu.make_async_copy(source, target, sems.at[6 + len(done)]))
+        done.append(pltpu.make_async_copy(source, target, sems.at[7 + len(done)]))
         done[-1].start()
 
     def put(field, values):
@@ -156,46 +162,29 @@
             for column, value in zip(columns, eig)
         ],
     )
+    copies[6].wait()
+    for column in columns:
+        here = slice(column, column + width)
+        other_ref[:, here] = dot3(dual, split(velocity_ref[here, :].T))
+        leave(other_ref.at[:, here], velocity_out.at[:, here])
     for copy in done:
         copy.wait()
 
 
-def velocity_kernel(velocity_ref, dual_ref, slope_ref, basis_ref, eig_ref, pairs_ref):
-    dual = split(dual_ref[...])
-    width = 256
-    for column in range(0, velocity_ref.shape[0], width):
-        eig_ref[:, column : column + width] = dot3(dual, split(velocity_ref[column : column + width, :].T))
-        slope = dot3(dual, split(slope_ref[:, column : column + width]))
-        pairs_ref[1, 0, :, column : column + width], pairs_ref[1, 1, :, column : column + width] = split(-slope)
-    pairs_ref[0, 0], pairs_ref[0, 1] = dual
-    pairs_ref[2, 0], pairs_ref[2, 1] = split(basis_ref[...])
-
-
-def plane_kernel(wide, narrow, recv_in, span_in, stream_in, send_out, recv_ref, send_ref, span_ref, stream_ref, sems):
-    copies = fetch(
-        [of_field(recv_in, 0), span_in, stream_in, of_field(recv_in, 1), of_field(recv_in, 2)],
-        [recv_ref.at[0], span_ref, stream_ref, recv_ref.at[1], recv_ref.at[2]],
-        sems,
-    )
-    done = []
-
-    def arrive(level, *which):
-        if level == 0:
-            for at in which:
-                copies[at].wait()
+def plane_kernel(wide, narrow, recv_ref, span_ref, stream_ref, send_ref):
+    received, sent = flat_rows(recv_ref), flat_rows(send_ref)
 
     def pair(ref):
         return ref[0], ref[1]
 
     lower = lax.broadcasted_iota(jnp.int32, (4 * wide, 128), 1) < 64
 
-    def rows(n, block, level):
-        return pl.ds(n * wide * 8 + block * 2 + level, wide, stride=8)
+    def rows(n, field, block, level):
+        return pl.ds(n * wide * 24 + field * 8 + block * 2 + level, wide, stride=24)
 
     def load(field, level):
-        held = field_rows(recv_ref, field)
         parts = [
-            jnp.concatenate([held[rows(n, block, level), :] for block in range(4)], axis=0)
+            jnp.concatenate([received[rows(n, field, block, level), :] for block in range(4)], axis=0)
             for n in range(narrow)
         ]
         turned = [pltpu.roll(part, 64, 1) for part in parts]
@@ -212,13 +201,10 @@
             second = dot3(pair(stream_ref.at[2 * at + 1]), field[1])
             return first + second, first - second
 
-        arrive(level, 0)
         phase = load(0, level)
-        arrive(level, 1, 2)
         spread = across(phase, 0)
         value, grad_x = ahead(spread, 0), ahead(spread, 1)
         grad_z = ahead(across(phase, 1), 0)
-        arrive(level, 3, 4)
         grad_y = ahead(across(load(1, level), 0), 0)
         lap = ahead(across(load(2, level), 0), 0)
         explicit, force_x, force_y, force_z = [], [], [], []
@@ -238,7 +224,6 @@
             )
 
         def put(field, even, odd):
-            held = field_rows(send_ref, field)
             for n in range(0, narrow, 2):
                 here = slice(n * 64, n * 64 + 128)
                 first, second = even[:, here], odd[:, here]
@@ -247,10 +232,7 @@
                     (n + 1, jnp.where(lower, pltpu.roll(first, 64, 1), second)),
                 ):
                     for block in range(4):
-                        held[rows(own, block, level), :] = value[block * wide : (block + 1) * wide]
-            if level == 1:
-                done.append(pltpu.make_async_copy(send_ref.at[field], of_field(send_out, field), sems.at[5 + field]))
-                done[-1].start()
+                        sent[rows(own, field, block, level), :] = value[block * wide : (block + 1) * wide]
 
         put(0, *[dot3(part, pair(span_ref.at[0])) for part in back(explicit, 0)])
         put(1, *[dot3(part, pair(span_ref.at[0])) for part in back(force_y, 0)])
@@ -264,30 +246,34 @@
 
     for level in range(2):
         one_level(level)
-    for copy in done:
-        copy.wait()
-
-
-def update_kernel(sizes, recv_in, eig_in, velocity_in, pairs_in, decay_in, phase_out, velocity_out, *scratch):
-    recv_ref, eig_ref, velocity_ref, pairs_ref, decay_ref, phase_ref, result_ref, sems = scratch
-    copies = fetch(
-        [of_field(recv_in, 0), pairs_in.at[0], of_field(recv_in, 1), of_field(recv_in, 2)]
-        + [pairs_in.at[1], decay_in, eig_in, velocity_in, pairs_in.at[2]],
-        [recv_ref.at[0], pairs_ref.at[0], recv_ref.at[1], recv_ref.at[2]]
-        + [pairs_ref.at[1], decay_ref, eig_ref, velocity_ref, pairs_ref.at[2]],
-        sems,
-    )
+
+
+def update_kernel(
+    sizes,
+    recv_ref,
+    eig_ref,
+    velocity_ref,
+    dual_ref,
+    slope_ref,
+    basis_ref,
+    decay_ref,
+    phase_out,
+    velocity_out,
+    phase_ref,
+    result_ref,
+    sems,
+):
     half = eig_ref.shape[0] // 2
     width = 256
     columns = range(0, eig_ref.shape[1], width)
 
     def get(field, column):
-        rows = field_rows(recv_ref, field)
+        rows = flat_rows(recv_ref)
         return jnp.concatenate(
             [
                 jnp.concatenate(
                     [
-                        rows[pl.ds((column // 128 + block) * 2 + level, half, stride=8), :]
+                        rows[pl.ds(field * 8 + (column // 128 + block) * 2 + level, half, stride=24), :]
                         for block in range(width // 128)
                     ],
                     axis=1,
@@ -297,26 +283,15 @@
             axis=0,
         )
 
-    def pair(at):
-        return pairs_ref[at, 0], pairs_ref[at, 1]
-
-    explicit, forcing = [], []
-    for column in columns:
-        if column == 0:
-            copies[0].wait()
-        value = split(get(0, column))
-        if column == 0:
-            copies[1].wait()
-        explicit.append(dot3(pair(0), value))
-        wave = wave_squared(column, width, *sizes)
-        if column == 0:
-            for copy in copies[2:5]:
-                copy.wait()
-        value = split(-wave * get(1, column))
-        other = split(get(2, column))
-        forcing.append(dot3(pair(0), value) + dot3(pair(1), other))
-    for copy in copies[5:]:
-        copy.wait()
+    dual = split(dual_ref[...])
+    slope = split(slope_ref[...])
+    basis = split(basis_ref[...])
+    explicit = [dot3(dual, split(get(0, column))) for column in columns]
+    forcing = [
+        -wave_squared(column, width, *sizes) * get(1, column) - dot3(slope, split(get(2, column)))
+        for column in columns
+    ]
+    forcing = [dot3(dual, split(value)) for value in forcing]
     decay = upright(decay_ref, width)
     done = []
     for at, column in enumerate(columns):
@@ -330,8 +305,8 @@
         for which, (value, ref, out) in enumerate(
             ((phase, phase_ref, phase_out), (velocity, result_ref, velocity_out))
         ):
-            ref[here, :] = dot3(pair(2), split(value)).T
-            done.append(pltpu.make_async_copy(ref.at[here], out.at[here], sems.at[9 + 2 * at + which]))
+            ref[here, :] = dot3(basis, split(value)).T
+            done.append(pltpu.make_async_copy(ref.at[here], out.at[here], sems.at[2 * at + which]))
             done[-1].start()
     for copy in done:
         copy.wait()
@@ -358,59 +333,50 @@
     count = rows_x * rows_z
     sizes = rows_x, rows_z, full_x, full_z
     square = jax.ShapeDtypeStruct((levels, count), f32)
-    flat = jax.ShapeDtypeStruct((wide * narrow, 24, 128), f32)
+    result = jax.ShapeDtypeStruct((count, levels), f32)
+    parts = jax.ShapeDtypeStruct((wide * narrow, 24, 128), f32)
     buffer = pltpu.VMEM((3, wide * narrow, 8, 128), f32)
-    pairs = jax.ShapeDtypeStruct((3, 2, levels, levels), bf16)
     held, line = pltpu.VMEM((levels, count), f32), pltpu.VMEM((1, levels), f32)
     sems = pltpu.SemaphoreType.DMA
     first = call(
         functools.partial(eigen_kernel, sizes),
-        [hbm] * 5,
-        [hbm, hbm],
-        [flat, square],
-        [buffer] + [held] * 4 + [line, held, sems((10,))],
-        3 * 6 * 512**3,
+        [hbm] * 6,
+        [hbm] * 3,
+        [parts, square, square],
+        [buffer] + [held] * 5 + [line, held, held, sems((13,))],
+        4 * 6 * 512**3,
         60,
     )
-    beside = call(velocity_kernel, [vmem] * 4, [vmem] * 2, [square, pairs], [], 2 * 6 * 512**3, 24)
     span, stream = (jnp.asarray(t) for t in (span_tables(full_z), stream_tables(full_x, wide)))
     planes = call(
-        functools.partial(plane_kernel, wide, narrow),
-        [hbm] * 3,
-        hbm,
-        flat,
-        [buffer, buffer, pltpu.VMEM(span.shape, bf16), pltpu.VMEM(stream.shape, bf16), sems((8,))],
-        204 * 2 * 256**3,
-        60,
+        functools.partial(plane_kernel, wide, narrow), [vmem] * 3, vmem, parts, [], 204 * 2 * 256**3, 40
     )
     last = call(
         functools.partial(update_kernel, sizes),
-        [hbm] * 5,
+        [vmem] * 7,
         [hbm] * 2,
-        [square] * 2,
-        [buffer] + [held] * 2
-        + [pltpu.VMEM(pairs.shape, bf16), line, held, held, sems((13,))],
+        [result] * 2,
+        [held, held, sems((4,))],
         5 * 6 * 512**3,
-        60,
-    )
-    return first, beside, lambda recv: planes(recv, span, stream), last
+        40,
+    )
+    return first, lambda recv: planes(recv, span, stream), last
 
 
 def body(phase, velocity, basis, dual_basis, wall_slope, decay_rates):
     rows_x, rows_z, levels = phase.shape
     wide, narrow = lax.axis_size("wide"), lax.axis_size("narrow")
-    first, beside, planes, last = stages(rows_x, rows_z, levels, wide, narrow)
+    first, planes, last = stages(rows_x, rows_z, levels, wide, narrow)
     decay = decay_rates.reshape(1, levels)
 
     def exchange(parts):
         return lax.all_to_all(parts, ("narrow", "wide"), split_axis=0, concat_axis=0, tiled=True)
 
-    send, phase_eig = first(phase.reshape(-1, levels), dual_basis, wall_slope, basis, decay)
-    velocity_eig, pairs = beside(velocity.reshape(-1, levels), dual_basis, wall_slope, basis)
-    recv = exchange(send)
-    recv, velocity_eig, pairs = lax.optimization_barrier((recv, velocity_eig, pairs))
-    recv = exchange(planes(recv))
-    outs = last(recv, phase_eig, velocity_eig, pairs, decay)
+    send, phase_eig, velocity_eig = first(
+        phase.reshape(-1, levels), velocity.reshape(-1, levels), dual_basis, wall_slope, basis, decay
+    )
+    recv = exchange(planes(exchange(send)))
+    outs = last(recv, phase_eig, velocity_eig, dual_basis, wall_slope, basis, decay)
     return tuple(out.reshape(phase.shape) for out in outs)
 
 

time: 202 us -> 195 us (0.965)
  blocking collectives: 82.1 us -> 172 us
  waiting for transfers between devices: 68.6 us -> 0 us
  starting transfers between devices: 15.3 us -> 0 us
  Pallas kernels: 30.6 us -> 22.5 us
  local copies, waits for them, and re-layouts: 3.85 us -> 0.05 us
    all_to_all x1 -> x2, blocking collectives: 82.1 us -> 172 us  [exchange(): lax.all_to_all(parts, ('narrow', 'wide'), split_axis=0, concat_axis=0, ti...]
    all_to_all x1 -> x0, waiting for transfers between devices: 68.6 us -> none  [exchange(): lax.all_to_all(parts, ('narrow', 'wide'), split_axis=0, concat_axis=0, ti...]
    all_to_all x1 -> x0, starting transfers between devices: 15.3 us -> none  [exchange(): lax.all_to_all(parts, ('narrow', 'wide'), split_axis=0, concat_axis=0, ti...]
    pallas_call x4 -> x3, Pallas kernels: 30.6 us -> 22.5 us  [the longest x1 9.45 us: stages(): return (first, lambda recv: planes(recv, span, stream), last)]
    unnamed x12 -> x16, local copies, waits for them, and re-layouts: 3.85 us -> 0.05 us
  transfers between devices with their start and end apart: 1 -> 0, of which waited for: 1 -> 0; matrix products, arithmetic and copies ran while one was open for 0% -> 0% of each run, Pallas kernels for 1% -> 0%
where the time goes in v1:
time: 195 us
  blocking collectives  172 us (88%)
  Pallas kernels  22.5 us (12%)
    all_to_all x2, blocking collectives, exchange(): lax.all_to_all(parts, ('narrow', 'wide'), split_axis=0, concat_axis=0, ti...  172 us
    pallas_call x1, Pallas kernels, stages(): return (first, lambda recv: planes(recv, span, stream), last)  9.45 us
    pallas_call x1, Pallas kernels, body(): first(phase.reshape(-1, levels), velocity.reshape(-1, levels), dual_basis...  7.11 us
    pallas_call x1, Pallas kernels, body(): last(recv, phase_eig, velocity_eig, dual_basis, wall_slope, basis, decay)  5.97 us

profile of v1, /device:TPU:32, one launch (start us, length us, event | category | flops | bytes accessed | tf_op | source)
XLA Modules:
  0.0 195.1 jit_solution(8908436040974619328)
XLA Ops:
  0.6 7.1 %shard_map.95 = (f32[256,24,128]{2,1,0:T(8,128)}, f32[512,512]{1,0:T(8,128)}, f32[512,512]{1,0:T(8,128)}) custom-call(f32[512,512]{1,0:T(8,128)} %bitcast.7, f32[512,512]{1,0:T(8,128)} %bitcast.8, f32[512,512]{1,0:T(8,128)} %dual_ref.1, f32[512,512]{1,0:T(8,128)} %slope_ref.1, f32[512,512]{1,0:T(8,128)} %basis_ref.1, f32[1,512]{1,0:T(1,128)} %bitcast.5), custom_call_target="tpu_custom_call" | custom-call | flops 3221225472 | bytes 4194304 | tf_op jit(solution)/shard_map/pallas_call | solution.py:375
  7.7 0.0 copy-start.4
  7.8 0.0 copy-start.5
  7.8 89.8 %all_to_all.10.recv_ref = f32[256,24,128]{2,1,0:T(8,128)S(1)} all-to-all(f32[256,24,128]{2,1,0:T(8,128)} %get-tuple-element.7), channel_id=1, replica_groups=mesh['wide'=64,'narrow'=4] {'narrow','wide'}, dimensions={0} | all-to-all | bytes 6291456 | tf_op jit(solution)/shard_map/all_to_all | solution.py:373
  97.6 0.0 copy-done.4
  97.6 0.0 copy-done.5
  97.6 9.5 %shard_map.96 = f32[256,24,128]{2,1,0:T(8,128)S(1)} custom-call(f32[256,24,128]{2,1,0:T(8,128)S(1)} %all_to_all.10.recv_ref, bf16[3,2,256,256]{3,2,1,0:T(8,128)(2,1)S(1)} %copy-done.5, bf16[8,2,256,256]{3,2,1,0:T(8,128)(2,1)S(1)} %copy-done.4), custom_call_target="tpu_custom_call" | custom-call | flops 6845104128 | bytes 4194304 | tf_op jit(solution)/shard_map/pallas_call | solution.py:363
  107.0 0.0 copy-start
  107.0 0.0 copy-start.1
  107.0 0.0 copy-start.2
  107.1 0.0 copy-start.3
  107.1 0.0 copy-start.6
  107.1 0.0 copy-start.7
  107.1 81.8 %all_to_all.11.recv_ref = f32[256,24,128]{2,1,0:T(8,128)S(1)} all-to-all(f32[256,24,128]{2,1,0:T(8,128)S(1)} %shard_map.96), channel_id=1, replica_groups=mesh['wide'=64,'narrow'=4] {'narrow','wide'}, dimensions={0} | all-to-all | bytes 6291456 | tf_op jit(solution)/shard_map/all_to_all | solution.py:373
  188.9 0.0 copy-done
  188.9 0.0 copy-done.1
  188.9 0.0 copy-done.2
  188.9 0.0 copy-done.3
  188.9 0.0 copy-done.6
  188.9 0.0 copy-done.7
  189.0 6.0 %shard_map.97 = (f32[512,512]{1,0:T(8,128)}, f32[512,512]{1,0:T(8,128)}) custom-call(f32[256,24,128]{2,1,0:T(8,128)S(1)} %all_to_all.11.recv_ref, f32[512,512]{1,0:T(8,128)S(1)} %copy-done.6, f32[512,512]{1,0:T(8,128)S(1)} %copy-done.7, f32[512,512]{1,0:T(8,128)S(1)} %copy-done, f32[512,512]{1,0:T(8,128)S(1)} %copy-done.1, f32[512,512]{1,0:T(8,128)S(1)} %copy-done.2, ...), custom_call_target="tpu_custom_call" | custom-call | flops 4026531840 | bytes 4194304 | tf_op jit(solution)/shard_map/pallas_call | solution.py:379
Async XLA Ops:
  7.7 89.8 %copy-start.4 = (bf16[8,2,256,256]{3,2,1,0:T(8,128)(2,1)S(1)}, bf16[8,2,256,256]{3,2,1,0:T(8,128)(2,1)}, u32[]{:S(2)}) copy-start(bf16[8,2,256,256]{3,2,1,0:T(8,128)(2,1)} %constant.5.clone.stream_ref) | copy-start | bytes 6291460
  7.8 89.8 %copy-start.5 = (bf16[3,2,256,256]{3,2,1,0:T(8,128)(2,1)S(1)}, bf16[3,2,256,256]{3,2,1,0:T(8,128)(2,1)}, u32[]{:S(2)}) copy-start(bf16[3,2,256,256]{3,2,1,0:T(8,128)(2,1)} %constant.4.clone.span_ref) | copy-start | bytes 2359300
  107.0 81.9 %copy-start = (f32[512,512]{1,0:T(8,128)S(1)}, f32[512,512]{1,0:T(8,128)}, u32[]{:S(2)}) copy-start(f32[512,512]{1,0:T(8,128)} %dual_ref.1) | copy-start | bytes 3145732
  107.0 81.9 %copy-start.1 = (f32[512,512]{1,0:T(8,128)S(1)}, f32[512,512]{1,0:T(8,128)}, u32[]{:S(2)}) copy-start(f32[512,512]{1,0:T(8,128)} %slope_ref.1) | copy-start | bytes 3145732
  107.0 81.9 %copy-start.2 = (f32[512,512]{1,0:T(8,128)S(1)}, f32[512,512]{1,0:T(8,128)}, u32[]{:S(2)}) copy-start(f32[512,512]{1,0:T(8,128)} %basis_ref.1) | copy-start | bytes 3145732
  107.1 81.9 %copy-start.3 = (f32[512]{0:T(512)S(1)}, f32[512]{0:T(512)}, u32[]{:S(2)}) copy-start(f32[512]{0:T(512)} %param.13) | copy-start | bytes 6148
  107.1 81.9 %copy-start.6 = (f32[512,512]{1,0:T(8,128)S(1)}, f32[512,512]{1,0:T(8,128)}, u32[]{:S(2)}) copy-start(f32[512,512]{1,0:T(8,128)} %get-tuple-element.8.eig_ref) | copy-start | bytes 3145732
  107.1 81.9 %copy-start.7 = (f32[512,512]{1,0:T(8,128)S(1)}, f32[512,512]{1,0:T(8,128)}, u32[]{:S(2)}) copy-start(f32[512,512]{1,0:T(8,128)} %get-tuple-element.9.velocity_ref) | copy-start | bytes 3145732

commit v2 on v1

--- a/solution.py
+++ b/solution.py
@@ -67,6 +67,12 @@
     return dot(left[0], right[0]) + (dot(left[0], right[1]) + dot(left[1], right[0]))
 
 
+def dot3_left(left, right):
+    rows = left[0].shape[0]
+    first = jnp.dot(jnp.concatenate([left[0], left[1]], axis=0), right[0], preferred_element_type=f32)
+    return first[:rows] + first[rows:] + jnp.dot(left[0], right[1], preferred_element_type=f32)
+
+
 def wave_squared(column, width, rows_x, rows_z, full_x, full_z):
     at = lax.broadcasted_iota(jnp.int32, (1, width), 1) + column
 
@@ -85,9 +91,9 @@
     return jnp.concatenate([turned] * (width // 128), axis=1)
 
 
-def fetch(sources, targets, sems):
+def fetch(sources, targets, sems, early):
     copies = [pltpu.make_async_copy(s, t, sems.at[at]) for at, (s, t) in enumerate(zip(sources, targets))]
-    for copy in copies:
+    for copy in copies[:early]:
         copy.start()
     return copies
 
@@ -106,23 +112,24 @@
 
 
 def eigen_kernel(
-    sizes, phase_in, velocity_in, dual_in, slope_in, basis_in, decay_in, send_out, eig_out, velocity_out, *scratch
+    sizes, phase_in, dual_in, slope_in, basis_in, decay_in, send_out, eig_out, *scratch
 ):
-    send_ref, phase_ref, velocity_ref, dual_ref, slope_ref, basis_ref, decay_ref, eig_ref, other_ref, sems = scratch
+    send_ref, phase_ref, dual_ref, slope_ref, basis_ref, decay_ref, eig_ref, sems = scratch
     levels = phase_ref.shape[1]
     half = levels // 2
     width = 256
     columns = range(0, phase_ref.shape[0], width)
     first, second = (pl.ds(column, width) for column in columns)
     copies = fetch(
-        [phase_in.at[first], phase_in.at[second], dual_in, slope_in, basis_in, decay_in, velocity_in],
-        [phase_ref.at[first], phase_ref.at[second], dual_ref, slope_ref, basis_ref, decay_ref, velocity_ref],
+        [phase_in.at[first], phase_in.at[second], dual_in, slope_in, basis_in, decay_in],
+        [phase_ref.at[first], phase_ref.at[second], dual_ref, slope_ref, basis_ref, decay_ref],
         sems,
+        3,
     )
     done = []
 
     def leave(source, target):
-        done.append(pltpu.make_async_copy(source, target, sems.at[7 + len(done)]))
+        done.append(pltpu.make_async_copy(source, target, sems.at[6 + len(done)]))
         done[-1].start()
 
     def put(field, values):
@@ -139,6 +146,9 @@
     turned = []
     for at, column in enumerate(columns):
         copies[at].wait()
+        if at == 0:
+            for copy in copies[3:]:
+                copy.start()
         turned.append(phase_ref[column : column + width, :].T)
     put(0, turned)
     pairs = [split(value) for value in turned]
@@ -155,18 +165,25 @@
     copies[5].wait()
     basis = split(basis_ref[...])
     decay = upright(decay_ref, width)
-    put(
-        2,
-        [
-            dot3(basis, split(-(decay + wave_squared(column, width, *sizes)) * value))
-            for column, value in zip(columns, eig)
-        ],
-    )
-    copies[6].wait()
-    for column in columns:
-        here = slice(column, column + width)
-        other_ref[:, here] = dot3(dual, split(velocity_ref[here, :].T))
-        leave(other_ref.at[:, here], velocity_out.at[:, here])
+    scaled = [
+        split(-(decay + wave_squared(column, width, *sizes)) * value) for column, value in zip(columns, eig)
+    ]
+    rows = field_rows(send_ref, 2)
+    part = half // 2
+    for own in range(2):
+        mine = [
+            jnp.concatenate([b[at : at + part] for at in (own * part, half + own * part)], axis=0) for b in basis
+        ]
+        for column, pair in zip(columns, scaled):
+            value = dot3(mine, pair)
+            for block in range(width // 128):
+                for level in range(2):
+                    row = own * part * 8 + (column // 128 + block) * 2 + level
+                    rows[pl.ds(row, part, stride=8), :] = value[
+                        level * part : (level + 1) * part, block * 128 : (block + 1) * 128
+                    ]
+        devices = slice(own * part, (own + 1) * part)
+        leave(send_ref.at[2, devices], send_out.at[devices, 16:24])
     for copy in done:
         copy.wait()
 
@@ -190,62 +207,87 @@
         turned = [pltpu.roll(part, 64, 1) for part in parts]
         even = [jnp.where(lower, parts[n], turned[n + 1]) for n in range(0, narrow, 2)]
         odd = [jnp.where(lower, turned[n], parts[n + 1]) for n in range(0, narrow, 2)]
-        return split(jnp.concatenate(even, axis=1)), split(jnp.concatenate(odd, axis=1))
-
-    def one_level(level):
-        def across(field, at):
-            return tuple(split(dot3(part, pair(span_ref.at[at]))) for part in field)
-
-        def ahead(field, at):
-            first = dot3(pair(stream_ref.at[2 * at]), field[0])
-            second = dot3(pair(stream_ref.at[2 * at + 1]), field[1])
-            return first + second, first - second
-
-        phase = load(0, level)
-        spread = across(phase, 0)
-        value, grad_x = ahead(spread, 0), ahead(spread, 1)
-        grad_z = ahead(across(phase, 1), 0)
-        grad_y = ahead(across(load(1, level), 0), 0)
-        lap = ahead(across(load(2, level), 0), 0)
-        explicit, force_x, force_y, force_z = [], [], [], []
-        for part in range(2):
-            v = value[part]
-            cubed = v * v * v
-            push = capillary * (cubed - v - interface_sq * lap[part])
-            explicit.append(cubed - (1.0 + stabilize) * v)
-            force_x.append(push * grad_x[part])
-            force_y.append(push * grad_y[part])
-            force_z.append(push * grad_z[part])
-
-        def back(value, at):
-            folded = value[0] + value[1], value[0] - value[1]
-            return tuple(
-                split(dot3(pair(stream_ref.at[4 + 2 * at + parity]), split(folded[parity]))) for parity in range(2)
+        return jnp.concatenate([jnp.concatenate(even, axis=1), jnp.concatenate(odd, axis=1)], axis=0)
+
+    half = 4 * wide
+
+    def across(values, at):
+        return split(dot3(values, pair(span_ref.at[at])))
+
+    def ahead(field, at):
+        first = dot3_left(pair(stream_ref.at[2 * at]), tuple(f[:half] for f in field))
+        second = dot3_left(pair(stream_ref.at[2 * at + 1]), tuple(f[half:] for f in field))
+        return first + second, first - second
+
+    def beside(pairs):
+        return tuple(jnp.concatenate(part, axis=1) for part in zip(*pairs))
+
+    def ahead_both(fields, at):
+        first = dot3_left(pair(stream_ref.at[2 * at]), beside([tuple(f[:half] for f in field) for field in fields]))
+        second = dot3_left(
+            pair(stream_ref.at[2 * at + 1]), beside([tuple(f[half:] for f in field) for field in fields])
+        )
+        points = first.shape[1] // 2
+        out = first + second, first - second
+        return [[o[:, :points] for o in out], [o[:, points:] for o in out]]
+
+    both = range(2)
+    phase = [split(load(0, level)) for level in both]
+    spread = [across(phase[level], 0) for level in both]
+    slope = [across(phase[level], 1) for level in both]
+    value = ahead_both(spread, 0)
+    rise = [split(load(1, level)) for level in both]
+    grad_x = ahead_both(spread, 1)
+    rise = [across(rise[level], 0) for level in both]
+    grad_z = ahead_both(slope, 0)
+    bend = [split(load(2, level)) for level in both]
+    grad_y = ahead_both(rise, 0)
+    bend = [across(bend[level], 0) for level in both]
+    lap = ahead_both(bend, 0)
+
+    def back(value, at):
+        folded = value[0] + value[1], value[0] - value[1]
+        return split(
+            jnp.concatenate(
+                [dot3_left(pair(stream_ref.at[4 + 2 * at + parity]), split(folded[parity])) for parity in range(2)],
+                axis=0,
             )
-
-        def put(field, even, odd):
-            for n in range(0, narrow, 2):
-                here = slice(n * 64, n * 64 + 128)
-                first, second = even[:, here], odd[:, here]
-                for own, value in (
-                    (n, jnp.where(lower, first, pltpu.roll(second, 64, 1))),
-                    (n + 1, jnp.where(lower, pltpu.roll(first, 64, 1), second)),
-                ):
-                    for block in range(4):
-                        sent[rows(own, field, block, level), :] = value[block * wide : (block + 1) * wide]
-
-        put(0, *[dot3(part, pair(span_ref.at[0])) for part in back(explicit, 0)])
-        put(1, *[dot3(part, pair(span_ref.at[0])) for part in back(force_y, 0)])
-        put(
-            2,
-            *[
-                dot3(a, pair(span_ref.at[0])) + dot3(b, pair(span_ref.at[2]))
-                for a, b in zip(back(force_x, 1), back(force_z, 0))
-            ],
         )
 
-    for level in range(2):
-        one_level(level)
+    def put(field, level, modes):
+        even, odd = modes[:half], modes[half:]
+        for n in range(0, narrow, 2):
+            here = slice(n * 64, n * 64 + 128)
+            first, second = even[:, here], odd[:, here]
+            for own, value in (
+                (n, jnp.where(lower, first, pltpu.roll(second, 64, 1))),
+                (n + 1, jnp.where(lower, pltpu.roll(first, 64, 1), second)),
+            ):
+                for block in range(4):
+                    sent[rows(own, field, block, level), :] = value[block * wide : (block + 1) * wide]
+
+    cubed = [[v * v * v for v in value[level]] for level in both]
+    explicit = [
+        [c - (1.0 + stabilize) * v for c, v in zip(cubed[level], value[level])] for level in both
+    ]
+    explicit = [back(explicit[level], 0) for level in both]
+    push = [
+        [capillary * (c - v - interface_sq * l) for c, v, l in zip(cubed[level], value[level], lap[level])]
+        for level in both
+    ]
+
+    def force(level, slopes):
+        return [p * g for p, g in zip(push[level], slopes[level])]
+
+    along = [back(force(level, grad_y), 0) for level in both]
+    for level in both:
+        put(0, level, dot3(explicit[level], pair(span_ref.at[0])))
+    spread = [back(force(level, grad_x), 1) for level in both]
+    for level in both:
+        put(1, level, dot3(along[level], pair(span_ref.at[0])))
+    slope = [back(force(level, grad_z), 0) for level in both]
+    for level in both:
+        put(2, level, dot3(spread[level], pair(span_ref.at[0])) + dot3(slope[level], pair(span_ref.at[2])))
 
 
 def update_kernel(
@@ -286,28 +328,38 @@
     dual = split(dual_ref[...])
     slope = split(slope_ref[...])
     basis = split(basis_ref[...])
+    decay = upright(decay_ref, width)
+    waves = [wave_squared(column, width, *sizes) for column in columns]
+    operators = [-(decay + wave) for wave in waves]
+    done = []
+
+    def leave(which, column, value):
+        ref, out = ((phase_ref, phase_out), (result_ref, velocity_out))[which]
+        here = slice(column, column + width)
+        ref[here, :] = value
+        done.append(pltpu.make_async_copy(ref.at[here], out.at[here], sems.at[len(done)]))
+        done[-1].start()
+
+    def new_phase(column, operator, explicit):
+        damping = 1.0 + time_step * mobility * -operator * (stabilize + interface_sq * -operator)
+        return (eig_ref[:, column : column + width] + time_step * mobility * operator * explicit) / damping
+
+    def new_velocity(operator, speed, forcing):
+        return (operator * speed + time_step * forcing) / (operator * (1.0 - time_step * viscosity * operator))
+
+    forcing = [dot3(slope, split(get(2, column))) for column in columns]
     explicit = [dot3(dual, split(get(0, column))) for column in columns]
-    forcing = [
-        -wave_squared(column, width, *sizes) * get(1, column) - dot3(slope, split(get(2, column)))
-        for column in columns
-    ]
-    forcing = [dot3(dual, split(value)) for value in forcing]
-    decay = upright(decay_ref, width)
-    done = []
-    for at, column in enumerate(columns):
-        here = slice(column, column + width)
-        operator = -(decay + wave_squared(column, width, *sizes))
-        damping = 1.0 + time_step * mobility * -operator * (stabilize + interface_sq * -operator)
-        phase = (eig_ref[:, here] + time_step * mobility * operator * explicit[at]) / damping
-        velocity = (operator * velocity_ref[:, here] + time_step * forcing[at]) / (
-            operator * (1.0 - time_step * viscosity * operator)
-        )
-        for which, (value, ref, out) in enumerate(
-            ((phase, phase_ref, phase_out), (velocity, result_ref, velocity_out))
-        ):
-            ref[here, :] = dot3(basis, split(value)).T
-            done.append(pltpu.make_async_copy(ref.at[here], out.at[here], sems.at[2 * at + which]))
-            done[-1].start()
+    forcing = [split(-wave * get(1, column) - value) for column, wave, value in zip(columns, waves, forcing)]
+    forcing = [dot3(dual, value) for value in forcing]
+    explicit = [split(new_phase(*at)) for at in zip(columns, operators, explicit)]
+    speed = [dot3(dual, split(velocity_ref[column : column + width, :].T)) for column in columns]
+    turned = split(basis_ref[...].T)
+    explicit = [dot3(tuple(v.T for v in value), turned) for value in explicit]
+    speed = [split(new_velocity(*at)) for at in zip(operators, speed, forcing)]
+    for column, value in zip(columns, explicit):
+        leave(0, column, value)
+    for column, value in zip(columns, speed):
+        leave(1, column, dot3(tuple(v.T for v in value), turned))
     for copy in done:
         copy.wait()
 
@@ -340,11 +392,11 @@
     sems = pltpu.SemaphoreType.DMA
     first = call(
         functools.partial(eigen_kernel, sizes),
-        [hbm] * 6,
-        [hbm] * 3,
-        [parts, square, square],
-        [buffer] + [held] * 5 + [line, held, held, sems((13,))],
-        4 * 6 * 512**3,
+        [hbm] * 5,
+        [hbm] * 2,
+        [parts, square],
+        [buffer] + [held] * 4 + [line, held, sems((11,))],
+        3 * 6 * 512**3,
         60,
     )
     span, stream = (jnp.asarray(t) for t in (span_tables(full_z), stream_tables(full_x, wide)))
@@ -372,11 +424,9 @@
     def exchange(parts):
         return lax.all_to_all(parts, ("narrow", "wide"), split_axis=0, concat_axis=0, tiled=True)
 
-    send, phase_eig, velocity_eig = first(
-        phase.reshape(-1, levels), velocity.reshape(-1, levels), dual_basis, wall_slope, basis, decay
-    )
+    send, phase_eig = first(phase.reshape(-1, levels), dual_basis, wall_slope, basis, decay)
     recv = exchange(planes(exchange(send)))
-    outs = last(recv, phase_eig, velocity_eig, dual_basis, wall_slope, basis, decay)
+    outs = last(recv, phase_eig, velocity.reshape(-1, levels), dual_basis, wall_slope, basis, decay)
     return tuple(out.reshape(phase.shape) for out in outs)
 
 

time: 195 us -> 193 us (0.990)
  no operation moved by 1% of the time
where the time goes in v2:
time: 193 us
  blocking collectives  172 us (89%)
  Pallas kernels  20.7 us (11%)
    all_to_all x2, blocking collectives, exchange(): lax.all_to_all(parts, ('narrow', 'wide'), split_axis=0, concat_axis=0, ti...  172 us
    pallas_call x1, Pallas kernels, stages(): return (first, lambda recv: planes(recv, span, stream), last)  8.27 us
    pallas_call x1, Pallas kernels, body(): last(recv, phase_eig, velocity.reshape(-1, levels), dual_basis, wall_slop...  6.51 us
    pallas_call x1, Pallas kernels, body(): first(phase.reshape(-1, levels), dual_basis, wall_slope, basis, decay)  5.92 us

profile of v2, /device:TPU:32, one launch (start us, length us, event | category | flops | bytes accessed | tf_op | source)
XLA Modules:
  0.0 193.2 jit_solution(2379706127498587120)
XLA Ops:
  0.6 5.9 %shard_map.95 = (f32[256,24,128]{2,1,0:T(8,128)}, f32[512,512]{1,0:T(8,128)}) custom-call(f32[512,512]{1,0:T(8,128)} %bitcast.8, f32[512,512]{1,0:T(8,128)} %dual_ref.1, f32[512,512]{1,0:T(8,128)} %slope_ref.1, f32[512,512]{1,0:T(8,128)} %basis_ref.1, f32[1,512]{1,0:T(1,128)} %bitcast.6), custom_call_target="tpu_custom_call" | custom-call | flops 2415919104 | bytes 4194304 | tf_op jit(solution)/shard_map/pallas_call | solution.py:427
  6.6 0.0 copy-start.5
  6.6 0.0 copy-start.6
  6.6 89.8 %all_to_all.10.recv_ref = f32[256,24,128]{2,1,0:T(8,128)S(1)} all-to-all(f32[256,24,128]{2,1,0:T(8,128)} %get-tuple-element.6), channel_id=1, replica_groups=mesh['wide'=64,'narrow'=4] {'narrow','wide'}, dimensions={0} | all-to-all | bytes 6291456 | tf_op jit(solution)/shard_map/all_to_all | solution.py:425
  96.4 0.0 copy-done.5
  96.4 0.0 copy-done.6
  96.4 8.3 %shard_map.96 = f32[256,24,128]{2,1,0:T(8,128)S(1)} custom-call(f32[256,24,128]{2,1,0:T(8,128)S(1)} %all_to_all.10.recv_ref, bf16[3,2,256,256]{3,2,1,0:T(8,128)(2,1)S(1)} %copy-done.6, bf16[8,2,256,256]{3,2,1,0:T(8,128)(2,1)S(1)} %copy-done.5), custom_call_target="tpu_custom_call" | custom-call | flops 6845104128 | bytes 4194304 | tf_op jit(solution)/shard_map/pallas_call | solution.py:415
  104.6 0.0 copy-start
  104.7 0.0 copy-start.1
  104.7 0.0 copy-start.2
  104.7 0.0 copy-start.3
  104.7 0.0 copy-start.4
  104.7 0.0 copy-start.7
  104.7 81.8 %all_to_all.11.recv_ref = f32[256,24,128]{2,1,0:T(8,128)S(1)} all-to-all(f32[256,24,128]{2,1,0:T(8,128)S(1)} %shard_map.96), channel_id=1, replica_groups=mesh['wide'=64,'narrow'=4] {'narrow','wide'}, dimensions={0} | all-to-all | bytes 6291456 | tf_op jit(solution)/shard_map/all_to_all | solution.py:425
  186.5 0.0 copy-done
  186.5 0.0 copy-done.1
  186.5 0.0 copy-done.2
  186.5 0.0 copy-done.3
  186.5 0.0 copy-done.4
  186.6 0.0 copy-done.7
  186.6 6.5 %shard_map.97 = (f32[512,512]{1,0:T(8,128)}, f32[512,512]{1,0:T(8,128)}) custom-call(f32[256,24,128]{2,1,0:T(8,128)S(1)} %all_to_all.11.recv_ref, f32[512,512]{1,0:T(8,128)S(1)} %copy-done.7, f32[512,512]{1,0:T(8,128)S(1)} %bitcast.5, f32[512,512]{1,0:T(8,128)S(1)} %copy-done, f32[512,512]{1,0:T(8,128)S(1)} %copy-done.1, f32[512,512]{1,0:T(8,128)S(1)} %copy-done.2, ...), custom_call_target="tpu_custom_call" | custom-call | flops 4026531840 | bytes 4194304 | tf_op jit(solution)/shard_map/pallas_call | solution.py:429
Async XLA Ops:
  6.6 89.8 %copy-start.5 = (bf16[8,2,256,256]{3,2,1,0:T(8,128)(2,1)S(1)}, bf16[8,2,256,256]{3,2,1,0:T(8,128)(2,1)}, u32[]{:S(2)}) copy-start(bf16[8,2,256,256]{3,2,1,0:T(8,128)(2,1)} %constant.5.clone.stream_ref) | copy-start | bytes 6291460
  6.6 89.8 %copy-start.6 = (bf16[3,2,256,256]{3,2,1,0:T(8,128)(2,1)S(1)}, bf16[3,2,256,256]{3,2,1,0:T(8,128)(2,1)}, u32[]{:S(2)}) copy-start(bf16[3,2,256,256]{3,2,1,0:T(8,128)(2,1)} %constant.4.clone.span_ref) | copy-start | bytes 2359300
  104.6 81.9 %copy-start = (f32[512,512]{1,0:T(8,128)S(1)}, f32[512,512]{1,0:T(8,128)}, u32[]{:S(2)}) copy-start(f32[512,512]{1,0:T(8,128)} %dual_ref.1) | copy-start | bytes 3145732
  104.7 81.9 %copy-start.1 = (f32[512,512]{1,0:T(8,128)S(1)}, f32[512,512]{1,0:T(8,128)}, u32[]{:S(2)}) copy-start(f32[512,512]{1,0:T(8,128)} %slope_ref.1) | copy-start | bytes 3145732
  104.7 81.9 %copy-start.2 = (f32[512,512]{1,0:T(8,128)S(1)}, f32[512,512]{1,0:T(8,128)}, u32[]{:S(2)}) copy-start(f32[512,512]{1,0:T(8,128)} %basis_ref.1) | copy-start | bytes 3145732
  104.7 81.9 %copy-start.3 = (f32[8,64,512]{2,1,0:T(8,128)S(1)}, f32[8,64,512]{2,1,0:T(8,128)}, u32[]{:S(2)}) copy-start(f32[8,64,512]{2,1,0:T(8,128)} %param.9) | copy-start | bytes 3145732
  104.7 81.9 %copy-start.4 = (f32[512]{0:T(512)S(1)}, f32[512]{0:T(512)}, u32[]{:S(2)}) copy-start(f32[512]{0:T(512)} %param.13) | copy-start | bytes 6148
  104.7 81.9 %copy-start.7 = (f32[512,512]{1,0:T(8,128)S(1)}, f32[512,512]{1,0:T(8,128)}, u32[]{:S(2)}) copy-start(f32[512,512]{1,0:T(8,128)} %get-tuple-element.7.eig_ref) | copy-start | bytes 3145732

commit v3 on v2

--- a/solution.py
+++ b/solution.py
@@ -124,7 +124,7 @@
         [phase_in.at[first], phase_in.at[second], dual_in, slope_in, basis_in, decay_in],
         [phase_ref.at[first], phase_ref.at[second], dual_ref, slope_ref, basis_ref, decay_ref],
         sems,
-        3,
+        4,
     )
     done = []
 
@@ -147,20 +147,20 @@
     for at, column in enumerate(columns):
         copies[at].wait()
         if at == 0:
-            for copy in copies[3:]:
+            for copy in copies[4:]:
                 copy.start()
         turned.append(phase_ref[column : column + width, :].T)
     put(0, turned)
     pairs = [split(value) for value in turned]
     copies[2].wait()
     dual = split(dual_ref[...])
-    eig = [dot3(dual, pair) for pair in pairs]
+    eig = [dot3_left(dual, pair) for pair in pairs]
     for column, value in zip(columns, eig):
         eig_ref[:, column : column + width] = value
     leave(eig_ref, eig_out)
     copies[3].wait()
     slope = split(slope_ref[...])
-    put(1, [dot3(slope, pair) for pair in pairs])
+    put(1, [dot3_left(slope, pair) for pair in pairs])
     copies[4].wait()
     copies[5].wait()
     basis = split(basis_ref[...])
@@ -175,7 +175,7 @@
             jnp.concatenate([b[at : at + part] for at in (own * part, half + own * part)], axis=0) for b in basis
         ]
         for column, pair in zip(columns, scaled):
-            value = dot3(mine, pair)
+            value = dot3_left(mine, pair)
             for block in range(width // 128):
                 for level in range(2):
                     row = own * part * 8 + (column // 128 + block) * 2 + level
@@ -347,17 +347,17 @@
     def new_velocity(operator, speed, forcing):
         return (operator * speed + time_step * forcing) / (operator * (1.0 - time_step * viscosity * operator))
 
-    forcing = [dot3(slope, split(get(2, column))) for column in columns]
-    explicit = [dot3(dual, split(get(0, column))) for column in columns]
+    forcing = [dot3_left(slope, split(get(2, column))) for column in columns]
+    explicit = [dot3_left(dual, split(get(0, column))) for column in columns]
     forcing = [split(-wave * get(1, column) - value) for column, wave, value in zip(columns, waves, forcing)]
-    forcing = [dot3(dual, value) for value in forcing]
     explicit = [split(new_phase(*at)) for at in zip(columns, operators, explicit)]
-    speed = [dot3(dual, split(velocity_ref[column : column + width, :].T)) for column in columns]
+    forcing = [dot3_left(dual, value) for value in forcing]
     turned = split(basis_ref[...].T)
-    explicit = [dot3(tuple(v.T for v in value), turned) for value in explicit]
+    explicit = [tuple(v.T for v in value) for value in explicit]
+    speed = [dot3_left(dual, split(velocity_ref[column : column + width, :].T)) for column in columns]
+    for column, value in zip(columns, explicit):
+        leave(0, column, dot3(value, turned))
     speed = [split(new_velocity(*at)) for at in zip(operators, speed, forcing)]
-    for column, value in zip(columns, explicit):
-        leave(0, column, value)
     for column, value in zip(columns, speed):
         leave(1, column, dot3(tuple(v.T for v in value), turned))
     for copy in done:

time: 193 us -> 193 us (level)
  no operation moved by 1% of the time
where the time goes in v3:
time: 193 us
  blocking collectives  172 us (89%)
  Pallas kernels  20.5 us (11%)
    all_to_all x2, blocking collectives, exchange(): lax.all_to_all(parts, ('narrow', 'wide'), split_axis=0, concat_axis=0, ti...  172 us
    pallas_call x1, Pallas kernels, stages(): return (first, lambda recv: planes(recv, span, stream), last)  8.27 us
    pallas_call x1, Pallas kernels, body(): last(recv, phase_eig, velocity.reshape(-1, levels), dual_basis, wall_slop...  6.42 us
    pallas_call x1, Pallas kernels, body(): first(phase.reshape(-1, levels), dual_basis, wall_slope, basis, decay)  5.86 us

profile of v3, /device:TPU:32, one launch (start us, length us, event | category | flops | bytes accessed | tf_op | source)
XLA Modules:
  0.0 193.1 jit_solution(18289010428572722962)
XLA Ops:
  0.6 5.9 %shard_map.95 = (f32[256,24,128]{2,1,0:T(8,128)}, f32[512,512]{1,0:T(8,128)}) custom-call(f32[512,512]{1,0:T(8,128)} %bitcast.8, f32[512,512]{1,0:T(8,128)} %dual_ref.1, f32[512,512]{1,0:T(8,128)} %slope_ref.1, f32[512,512]{1,0:T(8,128)} %basis_ref.1, f32[1,512]{1,0:T(1,128)} %bitcast.6), custom_call_target="tpu_custom_call" | custom-call | flops 2415919104 | bytes 4194304 | tf_op jit(solution)/shard_map/pallas_call | solution.py:427
  6.5 0.0 copy-start.5
  6.5 0.0 copy-start.6
  6.5 89.8 %all_to_all.10.recv_ref = f32[256,24,128]{2,1,0:T(8,128)S(1)} all-to-all(f32[256,24,128]{2,1,0:T(8,128)} %get-tuple-element.6), channel_id=1, replica_groups=mesh['wide'=64,'narrow'=4] {'narrow','wide'}, dimensions={0} | all-to-all | bytes 6291456 | tf_op jit(solution)/shard_map/all_to_all | solution.py:425
  96.3 0.0 copy-done.5
  96.3 0.0 copy-done.6
  96.3 8.3 %shard_map.96 = f32[256,24,128]{2,1,0:T(8,128)S(1)} custom-call(f32[256,24,128]{2,1,0:T(8,128)S(1)} %all_to_all.10.recv_ref, bf16[3,2,256,256]{3,2,1,0:T(8,128)(2,1)S(1)} %copy-done.6, bf16[8,2,256,256]{3,2,1,0:T(8,128)(2,1)S(1)} %copy-done.5), custom_call_target="tpu_custom_call" | custom-call | flops 6845104128 | bytes 4194304 | tf_op jit(solution)/shard_map/pallas_call | solution.py:415
  104.6 0.0 copy-start
  104.6 0.0 copy-start.1
  104.6 0.0 copy-start.2
  104.6 0.0 copy-start.3
  104.6 0.0 copy-start.4
  104.7 0.0 copy-start.7
  104.7 81.8 %all_to_all.11.recv_ref = f32[256,24,128]{2,1,0:T(8,128)S(1)} all-to-all(f32[256,24,128]{2,1,0:T(8,128)S(1)} %shard_map.96), channel_id=1, replica_groups=mesh['wide'=64,'narrow'=4] {'narrow','wide'}, dimensions={0} | all-to-all | bytes 6291456 | tf_op jit(solution)/shard_map/all_to_all | solution.py:425
  186.5 0.0 copy-done
  186.5 0.0 copy-done.1
  186.5 0.0 copy-done.2
  186.5 0.0 copy-done.3
  186.5 0.0 copy-done.4
  186.5 0.0 copy-done.7
  186.5 6.4 %shard_map.97 = (f32[512,512]{1,0:T(8,128)}, f32[512,512]{1,0:T(8,128)}) custom-call(f32[256,24,128]{2,1,0:T(8,128)S(1)} %all_to_all.11.recv_ref, f32[512,512]{1,0:T(8,128)S(1)} %copy-done.7, f32[512,512]{1,0:T(8,128)S(1)} %bitcast.5, f32[512,512]{1,0:T(8,128)S(1)} %copy-done, f32[512,512]{1,0:T(8,128)S(1)} %copy-done.1, f32[512,512]{1,0:T(8,128)S(1)} %copy-done.2, ...), custom_call_target="tpu_custom_call" | custom-call | flops 4026531840 | bytes 4194304 | tf_op jit(solution)/shard_map/pallas_call | solution.py:429
Async XLA Ops:
  6.5 89.8 %copy-start.5 = (bf16[8,2,256,256]{3,2,1,0:T(8,128)(2,1)S(1)}, bf16[8,2,256,256]{3,2,1,0:T(8,128)(2,1)}, u32[]{:S(2)}) copy-start(bf16[8,2,256,256]{3,2,1,0:T(8,128)(2,1)} %constant.5.clone.stream_ref) | copy-start | bytes 6291460
  6.5 89.8 %copy-start.6 = (bf16[3,2,256,256]{3,2,1,0:T(8,128)(2,1)S(1)}, bf16[3,2,256,256]{3,2,1,0:T(8,128)(2,1)}, u32[]{:S(2)}) copy-start(bf16[3,2,256,256]{3,2,1,0:T(8,128)(2,1)} %constant.4.clone.span_ref) | copy-start | bytes 2359300
  104.6 81.9 %copy-start = (f32[512,512]{1,0:T(8,128)S(1)}, f32[512,512]{1,0:T(8,128)}, u32[]{:S(2)}) copy-start(f32[512,512]{1,0:T(8,128)} %dual_ref.1) | copy-start | bytes 3145732
  104.6 81.9 %copy-start.1 = (f32[512,512]{1,0:T(8,128)S(1)}, f32[512,512]{1,0:T(8,128)}, u32[]{:S(2)}) copy-start(f32[512,512]{1,0:T(8,128)} %slope_ref.1) | copy-start | bytes 3145732
  104.6 81.9 %copy-start.2 = (f32[512,512]{1,0:T(8,128)S(1)}, f32[512,512]{1,0:T(8,128)}, u32[]{:S(2)}) copy-start(f32[512,512]{1,0:T(8,128)} %basis_ref.1) | copy-start | bytes 3145732
  104.6 81.9 %copy-start.3 = (f32[8,64,512]{2,1,0:T(8,128)S(1)}, f32[8,64,512]{2,1,0:T(8,128)}, u32[]{:S(2)}) copy-start(f32[8,64,512]{2,1,0:T(8,128)} %param.9) | copy-start | bytes 3145732
  104.6 81.9 %copy-start.4 = (f32[512]{0:T(512)S(1)}, f32[512]{0:T(512)}, u32[]{:S(2)}) copy-start(f32[512]{0:T(512)} %param.13) | copy-start | bytes 6148
  104.7 81.9 %copy-start.7 = (f32[512,512]{1,0:T(8,128)S(1)}, f32[512,512]{1,0:T(8,128)}, u32[]{:S(2)}) copy-start(f32[512,512]{1,0:T(8,128)} %get-tuple-element.7.eig_ref) | copy-start | bytes 3145732

commit v4 on v3

--- a/solution.py
+++ b/solution.py
@@ -212,7 +212,7 @@
     half = 4 * wide
 
     def across(values, at):
-        return split(dot3(values, pair(span_ref.at[at])))
+        return split(dot3_left(values, pair(span_ref.at[at])))
 
     def ahead(field, at):
         first = dot3_left(pair(stream_ref.at[2 * at]), tuple(f[:half] for f in field))
@@ -335,7 +335,7 @@
 
     def leave(which, column, value):
         ref, out = ((phase_ref, phase_out), (result_ref, velocity_out))[which]
-        here = slice(column, column + width)
+        here = slice(column, column + value.shape[0])
         ref[here, :] = value
         done.append(pltpu.make_async_copy(ref.at[here], out.at[here], sems.at[len(done)]))
         done[-1].start()
@@ -359,7 +359,9 @@
         leave(0, column, dot3(value, turned))
     speed = [split(new_velocity(*at)) for at in zip(operators, speed, forcing)]
     for column, value in zip(columns, speed):
-        leave(1, column, dot3(tuple(v.T for v in value), turned))
+        value = tuple(v.T for v in value)
+        for part in range(0, width, 128):
+            leave(1, column + part, dot3(tuple(v[part : part + 128] for v in value), turned))
     for copy in done:
         copy.wait()
 
@@ -408,7 +410,7 @@
         [vmem] * 7,
         [hbm] * 2,
         [result] * 2,
-        [held, held, sems((4,))],
+        [held, held, sems((6,))],
         5 * 6 * 512**3,
         40,
     )

time: 193 us -> 193 us (level)
  no operation moved by 1% of the time
where the time goes in v4:
time: 193 us
  blocking collectives  172 us (89%)
  Pallas kernels  20.5 us (11%)
    all_to_all x2, blocking collectives, exchange(): lax.all_to_all(parts, ('narrow', 'wide'), split_axis=0, concat_axis=0, ti...  172 us
    pallas_call x1, Pallas kernels, stages(): return (first, lambda recv: planes(recv, span, stream), last)  8.31 us
    pallas_call x1, Pallas kernels, body(): last(recv, phase_eig, velocity.reshape(-1, levels), dual_basis, wall_slop...  6.36 us
    pallas_call x1, Pallas kernels, body(): first(phase.reshape(-1, levels), dual_basis, wall_slope, basis, decay)  5.86 us

profile of v4, /device:TPU:32, one launch (start us, length us, event | category | flops | bytes accessed | tf_op | source)
XLA Modules:
  0.0 193.1 jit_solution(13505509956882805164)
XLA Ops:
  0.6 5.9 %shard_map.95 = (f32[256,24,128]{2,1,0:T(8,128)}, f32[512,512]{1,0:T(8,128)}) custom-call(f32[512,512]{1,0:T(8,128)} %bitcast.8, f32[512,512]{1,0:T(8,128)} %dual_ref.1, f32[512,512]{1,0:T(8,128)} %slope_ref.1, f32[512,512]{1,0:T(8,128)} %basis_ref.1, f32[1,512]{1,0:T(1,128)} %bitcast.6), custom_call_target="tpu_custom_call" | custom-call | flops 2415919104 | bytes 4194304 | tf_op jit(solution)/shard_map/pallas_call | solution.py:429
  6.5 0.0 copy-start.5
  6.5 0.0 copy-start.6
  6.5 89.8 %all_to_all.10.recv_ref = f32[256,24,128]{2,1,0:T(8,128)S(1)} all-to-all(f32[256,24,128]{2,1,0:T(8,128)} %get-tuple-element.6), channel_id=1, replica_groups=mesh['wide'=64,'narrow'=4] {'narrow','wide'}, dimensions={0} | all-to-all | bytes 6291456 | tf_op jit(solution)/shard_map/all_to_all | solution.py:427
  96.3 0.0 copy-done.5
  96.3 0.0 copy-done.6
  96.3 8.3 %shard_map.96 = f32[256,24,128]{2,1,0:T(8,128)S(1)} custom-call(f32[256,24,128]{2,1,0:T(8,128)S(1)} %all_to_all.10.recv_ref, bf16[3,2,256,256]{3,2,1,0:T(8,128)(2,1)S(1)} %copy-done.6, bf16[8,2,256,256]{3,2,1,0:T(8,128)(2,1)S(1)} %copy-done.5), custom_call_target="tpu_custom_call" | custom-call | flops 6845104128 | bytes 4194304 | tf_op jit(solution)/shard_map/pallas_call | solution.py:417
  104.6 0.0 copy-start
  104.6 0.0 copy-start.1
  104.7 0.0 copy-start.2
  104.7 0.0 copy-start.3
  104.7 0.0 copy-start.4
  104.7 0.0 copy-start.7
  104.7 81.8 %all_to_all.11.recv_ref = f32[256,24,128]{2,1,0:T(8,128)S(1)} all-to-all(f32[256,24,128]{2,1,0:T(8,128)S(1)} %shard_map.96), channel_id=1, replica_groups=mesh['wide'=64,'narrow'=4] {'narrow','wide'}, dimensions={0} | all-to-all | bytes 6291456 | tf_op jit(solution)/shard_map/all_to_all | solution.py:427
  186.5 0.0 copy-done
  186.5 0.0 copy-done.1
  186.5 0.0 copy-done.2
  186.5 0.0 copy-done.3
  186.5 0.0 copy-done.4
  186.5 0.0 copy-done.7
  186.6 6.4 %shard_map.97 = (f32[512,512]{1,0:T(8,128)}, f32[512,512]{1,0:T(8,128)}) custom-call(f32[256,24,128]{2,1,0:T(8,128)S(1)} %all_to_all.11.recv_ref, f32[512,512]{1,0:T(8,128)S(1)} %copy-done.7, f32[512,512]{1,0:T(8,128)S(1)} %bitcast.5, f32[512,512]{1,0:T(8,128)S(1)} %copy-done, f32[512,512]{1,0:T(8,128)S(1)} %copy-done.1, f32[512,512]{1,0:T(8,128)S(1)} %copy-done.2, ...), custom_call_target="tpu_custom_call" | custom-call | flops 4026531840 | bytes 4194304 | tf_op jit(solution)/shard_map/pallas_call | solution.py:431
Async XLA Ops:
  6.5 89.8 %copy-start.5 = (bf16[8,2,256,256]{3,2,1,0:T(8,128)(2,1)S(1)}, bf16[8,2,256,256]{3,2,1,0:T(8,128)(2,1)}, u32[]{:S(2)}) copy-start(bf16[8,2,256,256]{3,2,1,0:T(8,128)(2,1)} %constant.5.clone.stream_ref) | copy-start | bytes 6291460
  6.5 89.8 %copy-start.6 = (bf16[3,2,256,256]{3,2,1,0:T(8,128)(2,1)S(1)}, bf16[3,2,256,256]{3,2,1,0:T(8,128)(2,1)}, u32[]{:S(2)}) copy-start(bf16[3,2,256,256]{3,2,1,0:T(8,128)(2,1)} %constant.4.clone.span_ref) | copy-start | bytes 2359300
  104.6 81.9 %copy-start = (f32[512,512]{1,0:T(8,128)S(1)}, f32[512,512]{1,0:T(8,128)}, u32[]{:S(2)}) copy-start(f32[512,512]{1,0:T(8,128)} %dual_ref.1) | copy-start | bytes 3145732
  104.6 81.9 %copy-start.1 = (f32[512,512]{1,0:T(8,128)S(1)}, f32[512,512]{1,0:T(8,128)}, u32[]{:S(2)}) copy-start(f32[512,512]{1,0:T(8,128)} %slope_ref.1) | copy-start | bytes 3145732
  104.7 81.9 %copy-start.2 = (f32[512,512]{1,0:T(8,128)S(1)}, f32[512,512]{1,0:T(8,128)}, u32[]{:S(2)}) copy-start(f32[512,512]{1,0:T(8,128)} %basis_ref.1) | copy-start | bytes 3145732
  104.7 81.9 %copy-start.3 = (f32[8,64,512]{2,1,0:T(8,128)S(1)}, f32[8,64,512]{2,1,0:T(8,128)}, u32[]{:S(2)}) copy-start(f32[8,64,512]{2,1,0:T(8,128)} %param.9) | copy-start | bytes 3145732
  104.7 81.9 %copy-start.4 = (f32[512]{0:T(512)S(1)}, f32[512]{0:T(512)}, u32[]{:S(2)}) copy-start(f32[512]{0:T(512)} %param.13) | copy-start | bytes 6148
  104.7 81.9 %copy-start.7 = (f32[512,512]{1,0:T(8,128)S(1)}, f32[512,512]{1,0:T(8,128)}, u32[]{:S(2)}) copy-start(f32[512,512]{1,0:T(8,128)} %get-tuple-element.7.eig_ref) | copy-start | bytes 3145732

commit v5 on v4

--- a/solution.py
+++ b/solution.py
@@ -157,10 +157,10 @@
     eig = [dot3_left(dual, pair) for pair in pairs]
     for column, value in zip(columns, eig):
         eig_ref[:, column : column + width] = value
-    leave(eig_ref, eig_out)
     copies[3].wait()
     slope = split(slope_ref[...])
     put(1, [dot3_left(slope, pair) for pair in pairs])
+    leave(eig_ref, eig_out)
     copies[4].wait()
     copies[5].wait()
     basis = split(basis_ref[...])

time: 193 us -> 193 us (level)
  no operation moved by 1% of the time
where the time goes in v5:
time: 193 us
  blocking collectives  172 us (89%)
  Pallas kernels  20.5 us (11%)
    all_to_all x2, blocking collectives, exchange(): lax.all_to_all(parts, ('narrow', 'wide'), split_axis=0, concat_axis=0, ti...  172 us
    pallas_call x1, Pallas kernels, stages(): return (first, lambda recv: planes(recv, span, stream), last)  8.31 us
    pallas_call x1, Pallas kernels, body(): last(recv, phase_eig, velocity.reshape(-1, levels), dual_basis, wall_slop...  6.36 us
    pallas_call x1, Pallas kernels, body(): first(phase.reshape(-1, levels), dual_basis, wall_slope, basis, decay)  5.86 us

profile of v5, /device:TPU:32, one launch (start us, length us, event | category | flops | bytes accessed | tf_op | source)
XLA Modules:
  0.0 193.1 jit_solution(10341148702055613661)
XLA Ops:
  0.6 5.9 %shard_map.95 = (f32[256,24,128]{2,1,0:T(8,128)}, f32[512,512]{1,0:T(8,128)}) custom-call(f32[512,512]{1,0:T(8,128)} %bitcast.8, f32[512,512]{1,0:T(8,128)} %dual_ref.1, f32[512,512]{1,0:T(8,128)} %slope_ref.1, f32[512,512]{1,0:T(8,128)} %basis_ref.1, f32[1,512]{1,0:T(1,128)} %bitcast.6), custom_call_target="tpu_custom_call" | custom-call | flops 2415919104 | bytes 4194304 | tf_op jit(solution)/shard_map/pallas_call | solution.py:429
  6.5 0.0 copy-start.5
  6.5 0.0 copy-start.6
  6.5 89.8 %all_to_all.10.recv_ref = f32[256,24,128]{2,1,0:T(8,128)S(1)} all-to-all(f32[256,24,128]{2,1,0:T(8,128)} %get-tuple-element.6), channel_id=1, replica_groups=mesh['wide'=64,'narrow'=4] {'narrow','wide'}, dimensions={0} | all-to-all | bytes 6291456 | tf_op jit(solution)/shard_map/all_to_all | solution.py:427
  96.3 0.0 copy-done.5
  96.3 0.0 copy-done.6
  96.3 8.3 %shard_map.96 = f32[256,24,128]{2,1,0:T(8,128)S(1)} custom-call(f32[256,24,128]{2,1,0:T(8,128)S(1)} %all_to_all.10.recv_ref, bf16[3,2,256,256]{3,2,1,0:T(8,128)(2,1)S(1)} %copy-done.6, bf16[8,2,256,256]{3,2,1,0:T(8,128)(2,1)S(1)} %copy-done.5), custom_call_target="tpu_custom_call" | custom-call | flops 6845104128 | bytes 4194304 | tf_op jit(solution)/shard_map/pallas_call | solution.py:417
  104.6 0.0 copy-start
  104.6 0.0 copy-start.1
  104.7 0.0 copy-start.2
  104.7 0.0 copy-start.3
  104.7 0.0 copy-start.4
  104.7 0.0 copy-start.7
  104.7 81.8 %all_to_all.11.recv_ref = f32[256,24,128]{2,1,0:T(8,128)S(1)} all-to-all(f32[256,24,128]{2,1,0:T(8,128)S(1)} %shard_map.96), channel_id=1, replica_groups=mesh['wide'=64,'narrow'=4] {'narrow','wide'}, dimensions={0} | all-to-all | bytes 6291456 | tf_op jit(solution)/shard_map/all_to_all | solution.py:427
  186.5 0.0 copy-done
  186.5 0.0 copy-done.1
  186.5 0.0 copy-done.2
  186.5 0.0 copy-done.3
  186.5 0.0 copy-done.4
  186.5 0.0 copy-done.7
  186.6 6.4 %shard_map.97 = (f32[512,512]{1,0:T(8,128)}, f32[512,512]{1,0:T(8,128)}) custom-call(f32[256,24,128]{2,1,0:T(8,128)S(1)} %all_to_all.11.recv_ref, f32[512,512]{1,0:T(8,128)S(1)} %copy-done.7, f32[512,512]{1,0:T(8,128)S(1)} %bitcast.5, f32[512,512]{1,0:T(8,128)S(1)} %copy-done, f32[512,512]{1,0:T(8,128)S(1)} %copy-done.1, f32[512,512]{1,0:T(8,128)S(1)} %copy-done.2, ...), custom_call_target="tpu_custom_call" | custom-call | flops 4026531840 | bytes 4194304 | tf_op jit(solution)/shard_map/pallas_call | solution.py:431
Async XLA Ops:
  6.5 89.8 %copy-start.5 = (bf16[8,2,256,256]{3,2,1,0:T(8,128)(2,1)S(1)}, bf16[8,2,256,256]{3,2,1,0:T(8,128)(2,1)}, u32[]{:S(2)}) copy-start(bf16[8,2,256,256]{3,2,1,0:T(8,128)(2,1)} %constant.5.clone.stream_ref) | copy-start | bytes 6291460
  6.5 89.8 %copy-start.6 = (bf16[3,2,256,256]{3,2,1,0:T(8,128)(2,1)S(1)}, bf16[3,2,256,256]{3,2,1,0:T(8,128)(2,1)}, u32[]{:S(2)}) copy-start(bf16[3,2,256,256]{3,2,1,0:T(8,128)(2,1)} %constant.4.clone.span_ref) | copy-start | bytes 2359300
  104.6 81.9 %copy-start = (f32[512,512]{1,0:T(8,128)S(1)}, f32[512,512]{1,0:T(8,128)}, u32[]{:S(2)}) copy-start(f32[512,512]{1,0:T(8,128)} %dual_ref.1) | copy-start | bytes 3145732
  104.6 81.9 %copy-start.1 = (f32[512,512]{1,0:T(8,128)S(1)}, f32[512,512]{1,0:T(8,128)}, u32[]{:S(2)}) copy-start(f32[512,512]{1,0:T(8,128)} %slope_ref.1) | copy-start | bytes 3145732
  104.7 81.9 %copy-start.2 = (f32[512,512]{1,0:T(8,128)S(1)}, f32[512,512]{1,0:T(8,128)}, u32[]{:S(2)}) copy-start(f32[512,512]{1,0:T(8,128)} %basis_ref.1) | copy-start | bytes 3145732
  104.7 81.9 %copy-start.3 = (f32[8,64,512]{2,1,0:T(8,128)S(1)}, f32[8,64,512]{2,1,0:T(8,128)}, u32[]{:S(2)}) copy-start(f32[8,64,512]{2,1,0:T(8,128)} %param.9) | copy-start | bytes 3145732
  104.7 81.9 %copy-start.4 = (f32[512]{0:T(512)S(1)}, f32[512]{0:T(512)}, u32[]{:S(2)}) copy-start(f32[512]{0:T(512)} %param.13) | copy-start | bytes 6148
  104.7 81.9 %copy-start.7 = (f32[512,512]{1,0:T(8,128)S(1)}, f32[512,512]{1,0:T(8,128)}, u32[]{:S(2)}) copy-start(f32[512,512]{1,0:T(8,128)} %get-tuple-element.7.eig_ref) | copy-start | bytes 3145732
